TPU v7x, 32 devices: a whole 2x2x4 slice. The times are simulated.
32 devices in a mesh: tok: 8 (over y, x, core), kv: 4 (over z).
Axes of the slice: x: 2, y: 2, z: 4, core: 2. Of those that a mesh axis runs over, the one named last changes fastest.
Arguments:
- queries: bfloat16 [2048, 8192], P('tok', 'kv'), may hold values from -12 to 12
- key_states: bfloat16 [2048, 1024], P('tok', 'kv'), may hold values from -12 to 12
- value_states: bfloat16 [2048, 1024], P('tok', 'kv'), may hold values from -6 to 6
- doc_lengths: int32 [16], replicated, may hold values from 1 to 1024, 2048 in all
- block_plan: int32 [8, 8], replicated, may hold values from 0 to 7, each once within a row
Outputs:
- attention_out: bfloat16 [2048, 8192], P(('tok', 'kv'))
- served_lse: float32 [64, 2048], P('kv', 'tok')
Inputs may be any that keep to these rules, and one draw needn't show every extreme that they name: `doc_lengths`: positive lengths that sum to 2048; the largest is exactly 1024. Every row of block_plan is a permutation of 0 to 7.
All inputs are finite; a program needn't handle non-finite values.
Results may differ from a plain program's by a relative error of at most 0.012.
The roundings to bfloat16 on the way count: a program that leaves them out, or rounds other values in their place, can miss the bound.
Values may be sent and summed in bfloat16 or wider, within the bound.
No kernel may reach another device: no remote copies, remote signals or barrier semaphores. Data moves between devices by JAX's collectives and lax.ppermute only.
A program may use at most 64 MiB of HBM per device.

v0:
```python
from functools import partial
import math

import jax
import jax.numpy as jnp
from jax import lax
from jax.sharding import PartitionSpec as P

HEAD_DIM = 128


THETA = 500000.0
NEG = -1e30


def doc_layout(doc_lengths, token_index):
    doc_ends = jnp.cumsum(doc_lengths)
    passed = token_index[:, None] >= doc_ends[None, :]
    doc_ids = jnp.sum(passed.astype(jnp.int32), axis=1)
    starts = jnp.sum(jnp.where(passed, doc_lengths[None, :], 0), axis=1)
    return (doc_ids, token_index - starts)


def rotate(inputs, positions, heads):
    half_dim = HEAD_DIM // 2
    inv_freq = jnp.power(
        jnp.float32(THETA), -(jnp.arange(half_dim, dtype=jnp.float32) * 2.0 / HEAD_DIM)
    )
    angles = positions.astype(jnp.float32)[:, None] * inv_freq[None, :]
    cosine = jnp.cos(angles)[:, None, :]
    sine_val = jnp.sin(angles)[:, None, :]
    shaped = inputs.astype(jnp.float32).reshape(inputs.shape[0], heads, HEAD_DIM)
    leading = shaped[..., :half_dim]
    trailing = shaped[..., half_dim:]
    turned = jnp.concatenate(
        [leading * cosine - trailing * sine_val, trailing * cosine + leading * sine_val], axis=-1
    )
    return turned.reshape(inputs.shape[0], heads * HEAD_DIM).astype(jnp.bfloat16)


def attend_block(
    carry_state, query_rows, query_index, query_docs, key_rows, value_rows, key_index, key_docs
):
    row_max, row_sum, weighted = carry_state
    score_scale = 1.0 / math.sqrt(HEAD_DIM)
    scores = (
        jnp.einsum("rgqd,ngd->gqrn", query_rows, key_rows, preferred_element_type=jnp.float32)
        * score_scale
    )
    allowed = (
        (query_docs[:, None] == key_docs[None, :])
        & (key_index[None, :] <= query_index[:, None])
        & (key_index[None, :] >= 0)
    )
    scores = jnp.where(allowed, scores, NEG)
    new_max = jnp.maximum(row_max, jnp.max(scores, axis=-1))
    weights = jnp.where(allowed, jnp.exp(scores - new_max[..., None]), 0.0)
    factor = jnp.exp(row_max - new_max)
    row_sum = row_sum * factor + jnp.sum(weights, axis=-1)
    probs = weights.astype(jnp.bfloat16)
    weighted = weighted * factor[..., None] + jnp.einsum(
        "gqrn,ngd->gqrd", probs, value_rows, preferred_element_type=jnp.float32
    )
    return (new_max, row_sum, weighted)


def fold_keys(
    carry_state, piece, start, query_rows=None, query_index=None, query_docs=None, doc_lengths=None
):
    key_piece, value_piece = piece
    count = key_piece.shape[0]
    stride = math.gcd(count, 512)
    kv_local = key_piece.shape[1] // HEAD_DIM

    def inner(counter, running):
        offset = counter * stride
        key_rows = lax.dynamic_slice_in_dim(key_piece, offset, stride, 0).reshape(
            stride, kv_local, HEAD_DIM
        )
        value_rows = lax.dynamic_slice_in_dim(value_piece, offset, stride, 0).reshape(
            stride, kv_local, HEAD_DIM
        )
        key_index = offset + jnp.arange(stride, dtype=jnp.int32)
        key_docs, unused_pos = doc_layout(doc_lengths, key_index)
        return attend_block(
            running, query_rows, query_index, query_docs, key_rows, value_rows, key_index, key_docs
        )

    return lax.fori_loop(0, count // stride, inner, carry_state)


def finish(carry_state, rows, q_local):
    row_max, row_sum, weighted = carry_state
    mixed = weighted / row_sum[..., None]
    result = (
        jnp.transpose(mixed, (2, 0, 1, 3)).reshape(rows, q_local * HEAD_DIM).astype(jnp.bfloat16)
    )
    log_norm = (row_max + jnp.log(row_sum)).reshape(q_local, rows)
    return (result, log_norm)


def body(queries, key_states, value_states, doc_lengths, block_plan):
    shards = lax.axis_size("tok")
    shard_index = lax.axis_index("tok")
    tok_dev = queries.shape[0]
    block_rows = tok_dev // shards
    kv_local = key_states.shape[1] // HEAD_DIM
    q_local = queries.shape[1] // HEAD_DIM
    per_group = q_local // kv_local
    token_index = shard_index * tok_dev + jnp.arange(tok_dev, dtype=jnp.int32)
    doc_ids, positions = doc_layout(doc_lengths, token_index)
    q_rot = rotate(queries, positions, q_local)
    k_rot = rotate(key_states, positions, kv_local)
    my_blocks = lax.dynamic_index_in_dim(block_plan, shard_index, 0, keepdims=False)
    initial = (
        jnp.full((kv_local, per_group, tok_dev), NEG, jnp.float32),
        jnp.zeros((kv_local, per_group, tok_dev), jnp.float32),
        jnp.zeros((kv_local, per_group, tok_dev, HEAD_DIM), jnp.float32),
    )
    plan_column = lax.dynamic_index_in_dim(block_plan, shard_index, 1, keepdims=False)
    outgoing = jnp.take(q_rot.reshape(shards, block_rows, q_local * HEAD_DIM), my_blocks, axis=0)
    incoming = lax.all_to_all(outgoing, "tok", split_axis=0, concat_axis=0, tiled=True)
    served_index = (
        jnp.arange(shards, dtype=jnp.int32)[:, None] * tok_dev
        + plan_column[:, None] * block_rows
        + jnp.arange(block_rows, dtype=jnp.int32)[None, :]
    ).reshape(tok_dev)
    served_docs, unused_pos = doc_layout(doc_lengths, served_index)
    served_rows = incoming.reshape(tok_dev, kv_local, per_group, HEAD_DIM)
    folder = partial(
        fold_keys,
        query_rows=served_rows,
        query_index=served_index,
        query_docs=served_docs,
        doc_lengths=doc_lengths,
    )
    final_state = folder(
        initial,
        (
            lax.all_gather(k_rot, "tok", axis=0, tiled=True),
            lax.all_gather(value_states, "tok", axis=0, tiled=True),
        ),
        jnp.int32(0),
    )
    result, served_lse = finish(final_state, tok_dev, q_local)
    returned = lax.all_to_all(
        result.reshape(shards, block_rows, q_local * HEAD_DIM),
        "tok",
        split_axis=0,
        concat_axis=0,
        tiled=True,
    )
    ordered = (
        jnp.zeros_like(returned).at[my_blocks].set(returned).reshape(tok_dev, q_local * HEAD_DIM)
    )
    attention_out = lax.all_to_all(ordered, "kv", split_axis=0, concat_axis=1, tiled=True)
    return (attention_out, served_lse)


def solution(mesh):
    return jax.shard_map(
        body,
        mesh=mesh,
        in_specs=(P("tok", "kv"), P("tok", "kv"), P("tok", "kv"), P(), P()),
        out_specs=(P(("tok", "kv"), None), P("kv", "tok")),
        check_vma=False,
    )
```

profile of v0, /device:TPU:0, one launch (start us, length us, event | category | flops | bytes accessed | tf_op | source)
XLA Modules:
  0.0 209.6 jit_solution(17943025340976895711)
XLA Ops:
  7.2 1.5 add_reduce_fusion
  8.7 0.7 iota_add_fusion.2
  9.5 1.3 broadcast_in_dim.111
  10.8 1.3 select_reduce_fusion
  12.1 1.0 copy.47
  13.5 0.7 pad_maximum_fusion.1
  14.2 1.7 copy.36
  16.7 0.8 subtract_convert_fusion
  17.5 0.6 pad_maximum_fusion
  18.1 0.5 convert_element_type.53
  18.6 0.7 fusion.16
  19.3 0.5 copy-done.5
  19.8 0.6 gather_fusion
  20.5 0.7 compare_and_fusion
  21.2 1.1 broadcast_select_fusion
  22.3 5.2 %all-to-all-start = ((bf16[8,32,2048]{2,1,0:T(8,128)(2,1)}), bf16[8,32,2048]{2,1,0:T(8,128)(2,1)S(1)}, u32[]{:S(2)}, u32[]{:S(2)}) async-start(bf16[8,32,2048]{2,1,0:T(8,128)(2,1)} %broadcast_select_fusion), calls=%async_computation | async-start | bytes 2097152 | tf_op jit(solution)/shard_map/all_to_all | solution.py:122
  27.5 18.2 %all-to-all-done = bf16[8,32,2048]{2,1,0:T(8,128)(2,1)S(1)} async-done(((bf16[8,32,2048]{2,1,0:T(8,128)(2,1)}), bf16[8,32,2048]{2,1,0:T(8,128)(2,1)S(1)}, u32[]{:S(2)}, u32[]{:S(2)}) %all-to-all-start) | async-done | bytes 1048608 | tf_op jit(solution)/shard_map/all_to_all | solution.py:122
  46.2 25.6 %all-gather.5.cloned.1.call-done = bf16[2048,256]{0,1:T(8,128)(2,1)} async-done(((bf16[256,256]{0,1:T(8,128)(2,1)}), bf16[2048,256]{0,1:T(8,128)(2,1)}) %all-gather.5.cloned.1.call-update) | async-done | bytes 1048592 | tf_op jit(solution)/shard_map/all_gather | solution.py:141
  71.8 75.7 %while.20 = (s32[]{:T(128)}, f32[2,8,256]{2,1,0:T(8,128)S(1)}, f32[2,8,256]{2,1,0:T(8,128)}, f32[2,8,256,128]{3,2,1,0:T(8,128)S(1)}, s32[256]{0:T(256)}, /*index...) while((s32[]{:T(128)}, f32[2,8,256]{2,1,0:T(8,128)S(1)}, ...), condition=%wide.region_7.8_spmd.clone, body=%wide.region_3.7_spmd.clone.sunk | while | flops 1103148288 | bytes 66470268 | solution.py:89
  71.8 0.7 convert_reduce_fusion.3
  72.5 0.7 iota_add_fusion.6
  73.3 0.9 and_and_fusion.2
  74.2 1.1 constant_dynamic-slice_fusion.4
  75.3 5.3 %fusion.32 = (f32[2,8,256]{2,1,0:T(8,128)}, f32[2,512,256,8]{2,1,3,0:T(8,128)}) fusion(pred[256,512]{0,1:T(8,128)(4,1)S(1)} %and_and_fusion.2, bf16[512,2,128,1]{0,2,3,1:T(8,128)(2,1)S(1)} %bitcast.72, bf16[256,2,8,128]{3,0,2,1:T(8,128)(2,1)S(1)} %get-tuple-element.448), kind=kOutput, calls=%fused_computation.5.clone.1 | convolution fusion | flops 543158272 | bytes 9846784 | tf_op jit(solution)/shard_map/while/body/eval_jaxpr/rgqd,ngd->gqrn/dot_general | solution.py:47
  80.6 0.7 select_maximum_fusion.2
  81.4 4.6 %fusion.33 = f32[2,8,256]{2,1,0:T(8,128)S(1)} fusion(f32[2,512,256,8]{2,1,3,0:T(8,128)} %get-tuple-element.409, f32[2,8,256]{2,1,0:T(8,128)S(1)} %select_maximum_fusion.2, pred[256,512]{0,1:T(8,128)(4,1)S(1)} %and_and_fusion.2), kind=kLoop, calls=%fused_computation.7.clone.1 | loop fusion | flops 10481664 | bytes 8552448 | tf_op jit(solution)/shard_map/while/body/eval_jaxpr/reduce_sum | solution.py:59
  86.0 1.2 copy-done
  87.2 3.5 %fusion.35 = f32[2,8,256,128]{3,2,1,0:T(8,128)S(1)} fusion(f32[2,8,256,128]{3,2,1,0:T(8,128)S(1)} %get-tuple-element.430, bf16[512,2,128,1]{0,2,3,1:T(8,128)(2,1)S(1)} %bitcast.74, f32[2,512,256,8]{2,1,3,0:T(8,128)S(1)} %copy-done, f32[2,8,256]{2,1,0:T(8,128)S(1)} %select_maximum_fusion.2, pred[256,512]{0,1:T(8,128)(4,1)S(1)} %and_and_fusion.2, ...), kind=kOutput, calls=%fused_computation.11.clone.1 | convolution fusion | flops 548929536 | bytes 13008897 | tf_op jit(solution)/shard_map/while/body/eval_jaxpr/gqrn,ngd->gqrd/dot_general | solution.py:61
  90.7 0.7 convert_reduce_fusion.3
  91.4 0.7 iota_add_fusion.6
  92.2 0.9 and_and_fusion.2
  93.2 1.1 constant_dynamic-slice_fusion.4
  94.2 5.3 %fusion.32 = (f32[2,8,256]{2,1,0:T(8,128)}, f32[2,512,256,8]{2,1,3,0:T(8,128)}) fusion(pred[256,512]{0,1:T(8,128)(4,1)S(1)} %and_and_fusion.2, bf16[512,2,128,1]{0,2,3,1:T(8,128)(2,1)S(1)} %bitcast.72, bf16[256,2,8,128]{3,0,2,1:T(8,128)(2,1)S(1)} %get-tuple-element.448), kind=kOutput, calls=%fused_computation.5.clone.1 | convolution fusion | flops 543158272 | bytes 9846784 | tf_op jit(solution)/shard_map/while/body/eval_jaxpr/rgqd,ngd->gqrn/dot_general | solution.py:47
  99.6 0.7 select_maximum_fusion.2
  100.3 4.6 %fusion.33 = f32[2,8,256]{2,1,0:T(8,128)S(1)} fusion(f32[2,512,256,8]{2,1,3,0:T(8,128)} %get-tuple-element.409, f32[2,8,256]{2,1,0:T(8,128)S(1)} %select_maximum_fusion.2, pred[256,512]{0,1:T(8,128)(4,1)S(1)} %and_and_fusion.2), kind=kLoop, calls=%fused_computation.7.clone.1 | loop fusion | flops 10481664 | bytes 8552448 | tf_op jit(solution)/shard_map/while/body/eval_jaxpr/reduce_sum | solution.py:59
  104.9 1.2 copy-done
  106.1 3.5 %fusion.35 = f32[2,8,256,128]{3,2,1,0:T(8,128)S(1)} fusion(f32[2,8,256,128]{3,2,1,0:T(8,128)S(1)} %get-tuple-element.430, bf16[512,2,128,1]{0,2,3,1:T(8,128)(2,1)S(1)} %bitcast.74, f32[2,512,256,8]{2,1,3,0:T(8,128)S(1)} %copy-done, f32[2,8,256]{2,1,0:T(8,128)S(1)} %select_maximum_fusion.2, pred[256,512]{0,1:T(8,128)(4,1)S(1)} %and_and_fusion.2, ...), kind=kOutput, calls=%fused_computation.11.clone.1 | convolution fusion | flops 548929536 | bytes 13008897 | tf_op jit(solution)/shard_map/while/body/eval_jaxpr/gqrn,ngd->gqrd/dot_general | solution.py:61
  109.7 0.7 convert_reduce_fusion.3
  110.4 0.7 iota_add_fusion.6
  111.1 0.9 and_and_fusion.2
  112.1 1.1 constant_dynamic-slice_fusion.4
  113.2 5.3 %fusion.32 = (f32[2,8,256]{2,1,0:T(8,128)}, f32[2,512,256,8]{2,1,3,0:T(8,128)}) fusion(pred[256,512]{0,1:T(8,128)(4,1)S(1)} %and_and_fusion.2, bf16[512,2,128,1]{0,2,3,1:T(8,128)(2,1)S(1)} %bitcast.72, bf16[256,2,8,128]{3,0,2,1:T(8,128)(2,1)S(1)} %get-tuple-element.448), kind=kOutput, calls=%fused_computation.5.clone.1 | convolution fusion | flops 543158272 | bytes 9846784 | tf_op jit(solution)/shard_map/while/body/eval_jaxpr/rgqd,ngd->gqrn/dot_general | solution.py:47
  118.5 0.7 select_maximum_fusion.2
  119.2 4.6 %fusion.33 = f32[2,8,256]{2,1,0:T(8,128)S(1)} fusion(f32[2,512,256,8]{2,1,3,0:T(8,128)} %get-tuple-element.409, f32[2,8,256]{2,1,0:T(8,128)S(1)} %select_maximum_fusion.2, pred[256,512]{0,1:T(8,128)(4,1)S(1)} %and_and_fusion.2), kind=kLoop, calls=%fused_computation.7.clone.1 | loop fusion | flops 10481664 | bytes 8552448 | tf_op jit(solution)/shard_map/while/body/eval_jaxpr/reduce_sum | solution.py:59
  123.9 1.2 copy-done
  125.1 3.5 %fusion.35 = f32[2,8,256,128]{3,2,1,0:T(8,128)S(1)} fusion(f32[2,8,256,128]{3,2,1,0:T(8,128)S(1)} %get-tuple-element.430, bf16[512,2,128,1]{0,2,3,1:T(8,128)(2,1)S(1)} %bitcast.74, f32[2,512,256,8]{2,1,3,0:T(8,128)S(1)} %copy-done, f32[2,8,256]{2,1,0:T(8,128)S(1)} %select_maximum_fusion.2, pred[256,512]{0,1:T(8,128)(4,1)S(1)} %and_and_fusion.2, ...), kind=kOutput, calls=%fused_computation.11.clone.1 | convolution fusion | flops 548929536 | bytes 13008897 | tf_op jit(solution)/shard_map/while/body/eval_jaxpr/gqrn,ngd->gqrd/dot_general | solution.py:61
  128.6 0.7 convert_reduce_fusion.3
  129.3 0.7 iota_add_fusion.6
  130.1 0.9 and_and_fusion.2
  131.0 1.1 constant_dynamic-slice_fusion.4
  132.1 5.3 %fusion.32 = (f32[2,8,256]{2,1,0:T(8,128)}, f32[2,512,256,8]{2,1,3,0:T(8,128)}) fusion(pred[256,512]{0,1:T(8,128)(4,1)S(1)} %and_and_fusion.2, bf16[512,2,128,1]{0,2,3,1:T(8,128)(2,1)S(1)} %bitcast.72, bf16[256,2,8,128]{3,0,2,1:T(8,128)(2,1)S(1)} %get-tuple-element.448), kind=kOutput, calls=%fused_computation.5.clone.1 | convolution fusion | flops 543158272 | bytes 9846784 | tf_op jit(solution)/shard_map/while/body/eval_jaxpr/rgqd,ngd->gqrn/dot_general | solution.py:47
  137.4 0.7 select_maximum_fusion.2
  138.2 4.6 %fusion.33 = f32[2,8,256]{2,1,0:T(8,128)S(1)} fusion(f32[2,512,256,8]{2,1,3,0:T(8,128)} %get-tuple-element.409, f32[2,8,256]{2,1,0:T(8,128)S(1)} %select_maximum_fusion.2, pred[256,512]{0,1:T(8,128)(4,1)S(1)} %and_and_fusion.2), kind=kLoop, calls=%fused_computation.7.clone.1 | loop fusion | flops 10481664 | bytes 8552448 | tf_op jit(solution)/shard_map/while/body/eval_jaxpr/reduce_sum | solution.py:59
  142.8 1.2 copy-done
  144.0 3.5 %fusion.35 = f32[2,8,256,128]{3,2,1,0:T(8,128)S(1)} fusion(f32[2,8,256,128]{3,2,1,0:T(8,128)S(1)} %get-tuple-element.430, bf16[512,2,128,1]{0,2,3,1:T(8,128)(2,1)S(1)} %bitcast.74, f32[2,512,256,8]{2,1,3,0:T(8,128)S(1)} %copy-done, f32[2,8,256]{2,1,0:T(8,128)S(1)} %select_maximum_fusion.2, pred[256,512]{0,1:T(8,128)(4,1)S(1)} %and_and_fusion.2, ...), kind=kOutput, calls=%fused_computation.11.clone.1 | convolution fusion | flops 548929536 | bytes 13008897 | tf_op jit(solution)/shard_map/while/body/eval_jaxpr/gqrn,ngd->gqrd/dot_general | solution.py:61
  147.5 1.4 fusion.15
  149.0 0.7 copy.38
  150.2 17.9 %all_to_all.29 = bf16[8,32,2048]{2,1,0:T(8,128)(2,1)S(1)} all-to-all(bf16[8,32,2048]{2,1,0:T(8,128)(2,1)S(1)} %convert_element_type.56), channel_id=1, replica_groups=mesh['tok'=8,'kv'=4] {'tok'}, dimensions={0} | all-to-all | bytes 2097152 | tf_op jit(solution)/shard_map/all_to_all | solution.py:146
  168.1 1.1 broadcast_in_dim.107
  169.2 2.8 %scatter_fusion = bf16[8,32,2048]{2,1,0:T(8,128)(2,1)} fusion(bf16[8,32,2048]{2,1,0:T(8,128)(2,1)} %broadcast_in_dim.107, s32[8]{0:T(128)S(1)} %copy-done.6, bf16[8,32,2048]{2,1,0:T(8,128)(2,1)S(1)} %all_to_all.29), kind=kCustom, calls=%fused_computation.1 | custom fusion | bytes 3145760 | tf_op jit(solution)/shard_map/scatter | solution.py:154
  172.0 4.6 %all-to-all-start.2 = ((bf16[4,64,2048]{2,1,0:T(8,128)(2,1)}), bf16[4,64,2048]{2,1,0:T(8,128)(2,1)S(1)}, u32[]{:S(2)}, u32[]{:S(2)}) async-start(bf16[4,64,2048]{2,1,0:T(8,128)(2,1)} %bitcast.7), calls=%async_computation.2 | async-start | bytes 2097152 | tf_op jit(solution)/shard_map/all_to_all | solution.py:156
  176.6 0.6 add_bitcast_fusion
  177.2 24.5 %all-to-all-done.2 = bf16[4,64,2048]{2,1,0:T(8,128)(2,1)S(1)} async-done(((bf16[4,64,2048]{2,1,0:T(8,128)(2,1)}), bf16[4,64,2048]{2,1,0:T(8,128)(2,1)S(1)}, u32[]{:S(2)}, u32[]{:S(2)}) %all-to-all-start.2) | async-done | bytes 1048608 | tf_op jit(solution)/shard_map/all_to_all | solution.py:156
  201.7 1.1 copy.48
  (69 shorter events, 2.9 us)
Async XLA Ops:
  7.2 8.9 %copy-start.1 = (bf16[256,2048]{1,0:T(8,128)(2,1)S(1)}, bf16[256,2048]{1,0:T(8,128)(2,1)}, u32[]{:S(2)}) copy-start(bf16[256,2048]{1,0:T(8,128)(2,1)} %param.7) | copy-start | bytes 3145732
  7.2 39.1 %all-gather.3.cloned.1.call-start = ((), (), s32[]{:S(2)}) async-start(), calls=%async_computation.3 | async-start | bytes 1179648 | tf_op jit(solution)/shard_map/all_gather | solution.py:140
  14.2 57.6 %all-gather.5.cloned.1.call-start = ((), (), s32[]{:S(2)}) async-start(), calls=%async_computation.4 | async-start | bytes 1179648 | tf_op jit(solution)/shard_map/all_gather | solution.py:141
  19.3 0.5 copy-start.5
  22.3 23.4 %all-to-all-start = ((bf16[8,32,2048]{2,1,0:T(8,128)(2,1)}), bf16[8,32,2048]{2,1,0:T(8,128)(2,1)S(1)}, u32[]{:S(2)}, u32[]{:S(2)}) async-start(bf16[8,32,2048]{2,1,0:T(8,128)(2,1)} %broadcast_select_fusion), calls=%async_computation | async-start | bytes 2097152 | tf_op jit(solution)/shard_map/all_to_all | solution.py:122
  81.3 4.6 %copy-start.2 = (f32[2,8,256]{2,1,0:T(8,128)S(1)}, f32[2,8,256]{2,1,0:T(8,128)}, u32[]{:S(2)}) copy-start(f32[2,8,256]{2,1,0:T(8,128)} %get-tuple-element.429) | copy-start | bytes 49156 | tf_op jit(solution)/shard_map/while
  81.4 5.9 %copy-start = (f32[2,512,256,8]{2,1,3,0:T(8,128)S(1)}, f32[2,512,256,8]{2,1,3,0:T(8,128)}, u32[]{:S(2)}) copy-start(f32[2,512,256,8]{2,1,3,0:T(8,128)} %get-tuple-element.409) | copy-start | bytes 25165828 | tf_op jit(solution)/shard_map/while
  86.0 4.7 %copy-start.3 = (f32[2,8,256]{2,1,0:T(8,128)}, f32[2,8,256]{2,1,0:T(8,128)S(1)}, u32[]{:S(2)}) copy-start(f32[2,8,256]{2,1,0:T(8,128)S(1)} %get-tuple-element.443) | copy-start | bytes 49156 | tf_op jit(solution)/shard_map/while
  100.3 4.6 %copy-start.2 = (f32[2,8,256]{2,1,0:T(8,128)S(1)}, f32[2,8,256]{2,1,0:T(8,128)}, u32[]{:S(2)}) copy-start(f32[2,8,256]{2,1,0:T(8,128)} %get-tuple-element.429) | copy-start | bytes 49156 | tf_op jit(solution)/shard_map/while
  100.3 5.9 %copy-start = (f32[2,512,256,8]{2,1,3,0:T(8,128)S(1)}, f32[2,512,256,8]{2,1,3,0:T(8,128)}, u32[]{:S(2)}) copy-start(f32[2,512,256,8]{2,1,3,0:T(8,128)} %get-tuple-element.409) | copy-start | bytes 25165828 | tf_op jit(solution)/shard_map/while
  104.9 4.7 %copy-start.3 = (f32[2,8,256]{2,1,0:T(8,128)}, f32[2,8,256]{2,1,0:T(8,128)S(1)}, u32[]{:S(2)}) copy-start(f32[2,8,256]{2,1,0:T(8,128)S(1)} %get-tuple-element.443) | copy-start | bytes 49156 | tf_op jit(solution)/shard_map/while
  119.2 4.6 %copy-start.2 = (f32[2,8,256]{2,1,0:T(8,128)S(1)}, f32[2,8,256]{2,1,0:T(8,128)}, u32[]{:S(2)}) copy-start(f32[2,8,256]{2,1,0:T(8,128)} %get-tuple-element.429) | copy-start | bytes 49156 | tf_op jit(solution)/shard_map/while
  119.2 5.9 %copy-start = (f32[2,512,256,8]{2,1,3,0:T(8,128)S(1)}, f32[2,512,256,8]{2,1,3,0:T(8,128)}, u32[]{:S(2)}) copy-start(f32[2,512,256,8]{2,1,3,0:T(8,128)} %get-tuple-element.409) | copy-start | bytes 25165828 | tf_op jit(solution)/shard_map/while
  123.8 4.7 %copy-start.3 = (f32[2,8,256]{2,1,0:T(8,128)}, f32[2,8,256]{2,1,0:T(8,128)S(1)}, u32[]{:S(2)}) copy-start(f32[2,8,256]{2,1,0:T(8,128)S(1)} %get-tuple-element.443) | copy-start | bytes 49156 | tf_op jit(solution)/shard_map/while
  138.1 4.6 %copy-start.2 = (f32[2,8,256]{2,1,0:T(8,128)S(1)}, f32[2,8,256]{2,1,0:T(8,128)}, u32[]{:S(2)}) copy-start(f32[2,8,256]{2,1,0:T(8,128)} %get-tuple-element.429) | copy-start | bytes 49156 | tf_op jit(solution)/shard_map/while
  138.1 5.9 %copy-start = (f32[2,512,256,8]{2,1,3,0:T(8,128)S(1)}, f32[2,512,256,8]{2,1,3,0:T(8,128)}, u32[]{:S(2)}) copy-start(f32[2,512,256,8]{2,1,3,0:T(8,128)} %get-tuple-element.409) | copy-start | bytes 25165828 | tf_op jit(solution)/shard_map/while
  142.8 4.7 %copy-start.3 = (f32[2,8,256]{2,1,0:T(8,128)}, f32[2,8,256]{2,1,0:T(8,128)S(1)}, u32[]{:S(2)}) copy-start(f32[2,8,256]{2,1,0:T(8,128)S(1)} %get-tuple-element.443) | copy-start | bytes 49156 | tf_op jit(solution)/shard_map/while
  150.2 19.0 %copy-start.6 = (s32[8]{0:T(128)S(1)}, s32[8]{0:T(128)}, u32[]{:S(2)}) copy-start(s32[8]{0:T(128)} %copy-done.5) | copy-start | bytes 100
  169.2 7.4 %copy-start.4 = (f32[2,8,256]{2,1,0:T(8,128)S(1)}, f32[2,8,256]{2,1,0:T(8,128)}, u32[]{:S(2)}) copy-start(f32[2,8,256]{2,1,0:T(8,128)} %get-tuple-element.238) | copy-start | bytes 49156
  172.0 29.7 %all-to-all-start.2 = ((bf16[4,64,2048]{2,1,0:T(8,128)(2,1)}), bf16[4,64,2048]{2,1,0:T(8,128)(2,1)S(1)}, u32[]{:S(2)}, u32[]{:S(2)}) async-start(bf16[4,64,2048]{2,1,0:T(8,128)(2,1)} %bitcast.7), calls=%async_computation.2 | async-start | bytes 2097152 | tf_op jit(solution)/shard_map/all_to_all | solution.py:156
Sparse Core Ops, SparseCore 0:
  14.3 29.2 all-gather.2
  45.5 26.2 all-gather.4
where the time goes:
time: 211 us; the launch traced here: 210 us
  waiting for transfers between devices  68.3 us (32%)
  other arithmetic  42.5 us (20%)
  matrix products  35.3 us (17%)
  local copies, waits for them, and re-layouts  21.2 us (10%)
  blocking collectives  17.9 us (8%)
  between operations  14.2 us (7%)
  starting transfers between devices  9.85 us (5%)
    all_gather x1, waiting for transfers between devices, body(): lax.all_gather(value_states, 'tok', axis=0, tiled=True)  25.6 us
    all_to_all x1, waiting for transfers between devices, body(): lax.all_to_all(ordered, 'kv', split_axis=0, concat_axis=1, tiled=True)  24.5 us
    dot_general x4, matrix products, attend_block(): jnp.einsum('rgqd,ngd->gqrn', query_rows, key_rows, preferred_element_type...  21.3 us
    reduce_sum x4, other arithmetic, attend_block(): row_sum = row_sum * factor + jnp.sum(weights, axis=-1)  18.3 us
    all_to_all x1, waiting for transfers between devices, body(): lax.all_to_all(outgoing, 'tok', split_axis=0, concat_axis=0, tiled=True)  18.2 us
    all_to_all x1, blocking collectives, body(): lax.all_to_all(result.reshape(shards, block_rows, q_local * HEAD_DIM), 't...  17.9 us
    dot_general x4, matrix products, attend_block(): jnp.einsum('gqrn,ngd->gqrd', probs, value_rows, preferred_element_type=jn...  13.9 us
    all_to_all x1, starting transfers between devices, body(): lax.all_to_all(outgoing, 'tok', split_axis=0, concat_axis=0, tiled=True)  5.17 us
  transfers between devices with their start and end apart: 4, of which 3 were waited for; matrix products, arithmetic and copies ran while one was open for 4% of the time, Pallas kernels for 0%

commit v1 on v0

v1 whole, which is shorter than its diff:
```python
import math
from functools import partial

import jax
import jax.numpy as jnp
import numpy as np
from jax import lax
from jax.experimental import pallas as pl
from jax.experimental.pallas import tpu as pltpu
from jax.sharding import PartitionSpec as P

HEAD_DIM = 128
HALF = HEAD_DIM // 2
THETA = 500000.0
NEG = -1e30
LOG2E = math.log2(math.e)
SCALE = 1.0 / math.sqrt(HEAD_DIM)
VMEM_LIMIT = 48 * 1024 * 1024


def vmem():
    return pl.BlockSpec(memory_space=pltpu.VMEM)


def smem():
    return pl.BlockSpec(memory_space=pltpu.SMEM)


def hbm():
    return pl.BlockSpec(memory_space=pl.ANY)


def params():
    return pltpu.CompilerParams(vmem_limit_bytes=VMEM_LIMIT)


def doc_starts(lengths_ref, token):
    begin = jnp.int32(0)
    start = jnp.zeros_like(token)
    for doc in range(lengths_ref.shape[0] - 1):
        begin = begin + lengths_ref[doc]
        start = jnp.where(token >= begin, begin, start)
    return start


def rotary_tables(lengths_ref, freq_ref, rows, first):
    token = first + lax.broadcasted_iota(jnp.int32, (rows, HEAD_DIM), 0)
    position = token - doc_starts(lengths_ref, token)
    angle = position.astype(jnp.float32) * freq_ref[...]
    lane = lax.broadcasted_iota(jnp.int32, (rows, HEAD_DIM), 1)
    sine = jnp.sin(angle)
    return jnp.cos(angle), jnp.where(lane < HALF, -sine, sine)


def turn(block, cosine, sine):
    x = block.astype(jnp.float32)
    return (x * cosine + pltpu.roll(x, HALF, 1) * sine).astype(jnp.bfloat16)


def prepare_kernel(where_ref, lengths_ref, freq_ref, key_ref, value_ref, *out_refs):
    rows = key_ref.shape[0]
    cosine, sine = rotary_tables(lengths_ref, freq_ref, rows, where_ref[0] * rows)
    for group, out_ref in enumerate(out_refs):
        cols = pl.ds(group * HEAD_DIM, HEAD_DIM)
        out_ref[:, 0:HEAD_DIM] = turn(key_ref[:, cols], cosine, sine)
        out_ref[:, HEAD_DIM:] = value_ref[:, cols]


def queries_kernel(where_ref, lengths_ref, freq_ref, query_ref, *out_refs):
    rows = query_ref.shape[0]
    cosine, sine = rotary_tables(lengths_ref, freq_ref, rows, where_ref[0] * rows)
    tiles, stacked, _ = out_refs[0].shape
    tile = rows // tiles
    per_group = stacked // tile
    for group, out_ref in enumerate(out_refs):
        for head in range(per_group):
            cols = pl.ds((group * per_group + head) * HEAD_DIM, HEAD_DIM)
            turned = turn(query_ref[:, cols], cosine, sine)
            for t in range(tiles):
                out_ref[t, head * tile : (head + 1) * tile, :] = turned[t * tile : (t + 1) * tile]


def attend_kernel(pieces, per_group, where_ref, lengths_ref, query_ref, *refs):
    own_ref = refs[0]
    far_refs = refs[1 : 1 + pieces]
    near_refs = refs[1 + pieces : 2 + 2 * pieces]
    refs = refs[2 + 2 * pieces :]
    tiles = query_ref.shape[0]
    out_refs, lse_ref = refs[:tiles], refs[tiles]
    window, scores, sems = refs[tiles + 1 :]
    shard, z = where_ref[0], where_ref[1]
    rows = own_ref.shape[0]
    tile = rows // tiles
    slots = 2 * pieces + 1
    odd = lax.rem(shard, 2) == 1

    def copy(ref, slot):
        return pltpu.make_async_copy(ref, window.at[slot], sems.at[slot])

    fixed = [copy(own_ref, slots - 1)]
    for i in range(1, pieces + 1):
        fixed.append(copy(far_refs[i - 1], slots - 1 - 2 * i))
    for c in fixed:
        c.start()
    for i in range(1, pieces + 1):
        slot = slots - 2 * i

        @pl.when(odd)
        def _():
            copy(near_refs[i - 1], slot).start()

        @pl.when(jnp.logical_not(odd))
        def _():
            copy(near_refs[i], slot).start()

    for c in fixed:
        c.wait()
    for i in range(1, pieces + 1):
        copy(near_refs[i], slots - 2 * i).wait()

    window_first = (shard - (slots - 1)) * rows
    exponent = SCALE * LOG2E
    for s in range(tiles):
        t = lax.rem(z + s, tiles)
        first = shard * rows + t * tile
        token = first + lax.broadcasted_iota(jnp.int32, (tile, rows), 0)
        start = doc_starts(lengths_ref, token)
        lowest = jnp.int32(0)
        begin = jnp.int32(0)
        for doc in range(lengths_ref.shape[0] - 1):
            begin = begin + lengths_ref[doc]
            lowest = jnp.where(first >= begin, begin, lowest)
        low_slot = (lowest - window_first) // rows
        column = lax.broadcasted_iota(jnp.int32, (tile, rows), 1)

        def score_step(slot, highest):
            key = window_first + slot * rows + column
            allowed = (key >= start) & (key <= token)
            keys = window[slot, :, 0:HEAD_DIM]
            result = []
            for head in range(per_group):
                q = query_ref[t, head * tile : (head + 1) * tile, :]
                block = lax.dot_general(
                    q, keys, (((1,), (1,)), ((), ())), preferred_element_type=jnp.float32
                )
                block = jnp.where(allowed, block, NEG)
                scores[slot, head * tile : (head + 1) * tile, :] = block
                best = highest[head]
                for lane in range(0, rows, HEAD_DIM):
                    best = jnp.maximum(best, block[:, lane : lane + HEAD_DIM])
                result.append(best)
            return tuple(result)

        highest = lax.fori_loop(
            low_slot,
            slots,
            score_step,
            tuple(jnp.full((tile, HEAD_DIM), NEG, jnp.float32) for _ in range(per_group)),
        )
        row_max = [jnp.max(h, axis=1, keepdims=True) for h in highest]
        shift = [jnp.broadcast_to(m * exponent, (tile, rows)) for m in row_max]

        def value_step(slot, state):
            sums, totals = state
            values = window[slot, :, HEAD_DIM:]
            new_sums, new_totals = [], []
            for head in range(per_group):
                block = scores[slot, head * tile : (head + 1) * tile, :]
                weights = jnp.exp2(block * exponent - shift[head])
                partial_sum = sums[head]
                for lane in range(0, rows, HEAD_DIM):
                    partial_sum = partial_sum + weights[:, lane : lane + HEAD_DIM]
                new_sums.append(partial_sum)
                new_totals.append(
                    totals[head]
                    + jnp.dot(
                        weights.astype(jnp.bfloat16), values, preferred_element_type=jnp.float32
                    )
                )
            return tuple(new_sums), tuple(new_totals)

        zeros = tuple(jnp.zeros((tile, HEAD_DIM), jnp.float32) for _ in range(per_group))
        sums, totals = lax.fori_loop(low_slot, slots, value_step, (zeros, zeros))
        norms = []
        for head in range(per_group):
            row_sum = jnp.sum(sums[head], axis=1, keepdims=True)
            out_refs[s][:, head * HEAD_DIM : (head + 1) * HEAD_DIM] = (
                totals[head] / row_sum
            ).astype(jnp.bfloat16)
            norms.append(row_max[head] * SCALE + jnp.log(row_sum))
        lse_ref[t] = jnp.concatenate(norms, axis=1)


def assemble_kernel(shards, groups, where_ref, *refs):
    pieces, out_ref, sems = refs[:-2], refs[-2], refs[-1]
    z = where_ref[1]
    width = pieces[0].shape[1]
    copies = []
    for s in range(shards):
        origin = lax.rem(z - s + shards, shards)
        for group in range(groups):
            column = pl.multiple_of((origin * groups + group) * width, width)
            index = s * groups + group
            copies.append(
                pltpu.make_async_copy(
                    pieces[index], out_ref.at[:, pl.ds(column, width)], sems.at[index]
                )
            )
    for c in copies:
        c.start()
    for c in copies:
        c.wait()


def body(queries, key_states, value_states, doc_lengths, block_plan):
    shards = lax.axis_size("tok")
    planes = lax.axis_size("kv")
    shard = lax.axis_index("tok")
    z = lax.axis_index("kv")
    rows = queries.shape[0]
    groups = key_states.shape[1] // HEAD_DIM
    heads = queries.shape[1] // HEAD_DIM
    per_group = heads // groups
    tile = rows // planes
    pieces = shards // 4
    where = jnp.stack([shard, z]).astype(jnp.int32)
    half_freq = THETA ** (-np.arange(HALF, dtype=np.float64) * 2.0 / HEAD_DIM)
    freq = jnp.asarray(np.concatenate([half_freq, half_freq])[None, :], jnp.float32)

    with jax.named_scope("rotate_keys"):
        packed = pl.pallas_call(
            prepare_kernel,
            out_shape=[jax.ShapeDtypeStruct((rows, 2 * HEAD_DIM), jnp.bfloat16)] * groups,
            in_specs=[smem(), smem(), vmem(), vmem(), vmem()],
            out_specs=[vmem()] * groups,
            compiler_params=params(),
        )(where, doc_lengths, freq, key_states, value_states)
    with jax.named_scope("rotate_queries"):
        turned = pl.pallas_call(
            queries_kernel,
            out_shape=[
                jax.ShapeDtypeStruct((planes, per_group * tile, HEAD_DIM), jnp.bfloat16)
            ]
            * groups,
            in_specs=[smem(), smem(), vmem(), vmem()],
            out_specs=[vmem()] * groups,
            compiler_params=params(),
        )(where, doc_lengths, freq, queries)

    pair = [(i, i ^ 1) for i in range(shards)]
    to_odd = [(i, i + 1) for i in range(0, shards, 2)]
    to_even = [(i + 1, i) for i in range(0, shards, 2)]
    outs, norms = [], []
    previous = None
    for group in range(groups):
        own = packed[group]
        if previous is not None:
            own, _ = lax.optimization_barrier((own, previous))
        far = [
            lax.ppermute(own, "tok", [(i, i + 2 * p) for i in range(shards - 2 * p)])
            for p in range(1, pieces + 1)
        ]
        previous = far
        near = [lax.ppermute(own, "tok", to_odd)]
        for p in range(1, pieces):
            near.append(lax.ppermute(far[p - 1], "tok", pair))
        near.append(lax.ppermute(far[pieces - 1], "tok", to_even))
        with jax.named_scope("attend"):
            result = pl.pallas_call(
                partial(attend_kernel, pieces, per_group),
                out_shape=[jax.ShapeDtypeStruct((tile, per_group * HEAD_DIM), jnp.bfloat16)]
                * planes
                + [jax.ShapeDtypeStruct((planes, tile, per_group), jnp.float32)],
                in_specs=[smem(), smem(), vmem()] + [hbm()] * (2 + 2 * pieces),
                out_specs=[vmem()] * (planes + 1),
                scratch_shapes=[
                    pltpu.VMEM((2 * pieces + 1, rows, 2 * HEAD_DIM), jnp.bfloat16),
                    pltpu.VMEM((2 * pieces + 1, per_group * tile, rows), jnp.float32),
                    pltpu.SemaphoreType.DMA((2 * pieces + 1,)),
                ],
                compiler_params=params(),
            )(where, doc_lengths, turned[group], own, *far, *near)
        outs.append(result[:planes])
        norms.append(result[planes])

    received = []
    for group in range(groups):
        row = [outs[group][0]]
        for s in range(1, planes):
            row.append(
                lax.ppermute(
                    outs[group][s], "kv", [(i, (i + s) % planes) for i in range(planes)]
                )
            )
        received.append(row)
    flat = [received[g][s] for s in range(planes) for g in range(groups)]
    with jax.named_scope("assemble"):
        attention_out = pl.pallas_call(
            partial(assemble_kernel, planes, groups),
            out_shape=jax.ShapeDtypeStruct((tile, planes * heads * HEAD_DIM), jnp.bfloat16),
            in_specs=[smem()] + [hbm()] * len(flat),
            out_specs=hbm(),
            scratch_shapes=[pltpu.SemaphoreType.DMA((len(flat),))],
            compiler_params=params(),
        )(where, *flat)

    block_rows = rows // shards
    log_norm = jnp.concatenate([n.reshape(rows, per_group) for n in norms], axis=1)
    my_blocks = lax.dynamic_index_in_dim(block_plan, shard, 0, keepdims=False)
    outgoing = jnp.take(log_norm.reshape(shards, block_rows, heads), my_blocks, axis=0)
    served = lax.all_to_all(outgoing, "tok", split_axis=0, concat_axis=0, tiled=True)
    served_lse = served.reshape(rows, heads).T
    return (attention_out, served_lse)


def solution(mesh):
    return jax.shard_map(
        body,
        mesh=mesh,
        in_specs=(P("tok", "kv"), P("tok", "kv"), P("tok", "kv"), P(), P()),
        out_specs=(P(("tok", "kv"), None), P("kv", "tok")),
        check_vma=False,
    )
```

time: 211 us -> 78.8 us (0.37)
  waiting for transfers between devices: 68.3 us -> 1.75 us
  other arithmetic: 42.5 us -> 2.25 us
  matrix products: 35.3 us -> 0 us
  starting transfers between devices: 9.85 us -> 31.2 us
  Pallas kernels: 0 us -> 15.5 us
  local copies, waits for them, and re-layouts: 21.2 us -> 5.72 us
  between operations: 14.2 us -> 0.89 us
  blocking collectives: 17.9 us -> 21.1 us
    all_to_all x2 -> x0, waiting for transfers between devices: 42.7 us -> none  [the longest x1 24.5 us: body(): lax.all_to_all(ordered, 'kv', split_axis=0, concat_axis=1, tiled=True)]
    dot_general x8 -> x0, matrix products: 35.3 us -> none  [the longest x4 21.3 us: attend_block(): jnp.einsum('rgqd,ngd->gqrn', query_rows, key_rows, preferred_element_type...]
    ppermute x0 -> x16, starting transfers between devices: none -> 31.2 us  [the longest x4 14.6 us: body(): lax.ppermute(own, 'tok', [(i, i + 2 * p) for i in range(shards - 2 * p)])]
    all_gather x2 -> x0, waiting for transfers between devices: 25.6 us -> none  [the longest x1 25.6 us: body(): lax.all_gather(value_states, 'tok', axis=0, tiled=True)]
    reduce_sum x9 -> x0, other arithmetic: 22.4 us -> none  [the longest x4 18.3 us: attend_block(): row_sum = row_sum * factor + jnp.sum(weights, axis=-1)]
    pallas_call x0 -> x5, Pallas kernels: none -> 15.5 us  [the longest x2 10.9 us: body(): pl.pallas_call(partial(attend_kernel, pieces, per_group), out_shape=[jax....]
    all_to_all x2 -> x0, starting transfers between devices: 9.77 us -> none  [the longest x1 5.17 us: body(): lax.all_to_all(outgoing, 'tok', split_axis=0, concat_axis=0, tiled=True)]
    while x28 -> x0, local copies, waits for them, and re-layouts: 4.93 us -> none
  transfers between devices with their start and end apart: 4 -> 16, of which waited for: 3 -> 1; matrix products, arithmetic and copies ran while one was open for 4% -> 5% of each run, Pallas kernels for 0% -> 16%
where the time goes in v1:
time: 78.8 us; the launch traced here: 78.3 us
  starting transfers between devices  31.2 us (40%)
  blocking collectives  21.1 us (27%)
  Pallas kernels  15.5 us (20%)
  local copies, waits for them, and re-layouts  5.72 us (7%)
  other arithmetic  2.25 us (3%)
  waiting for transfers between devices  1.75 us (2%)
  between operations  0.89 us (1%)
    all_to_all x1, blocking collectives, body(): lax.all_to_all(outgoing, 'tok', split_axis=0, concat_axis=0, tiled=True)  21.1 us
    ppermute x4, starting transfers between devices, body(): lax.ppermute(own, 'tok', [(i, i + 2 * p) for i in range(shards - 2 * p)])  14.6 us
    pallas_call x2, Pallas kernels, body(): pl.pallas_call(partial(attend_kernel, pieces, per_group), out_shape=[jax....  10.9 us
    ppermute x6, starting transfers between devices, body(): lax.ppermute(outs[group][s], 'kv', [(i, (i + s) % planes) for i in range(...  9.54 us
    ppermute x2, starting transfers between devices, body(): near = [lax.ppermute(own, 'tok', to_odd)]  4.33 us
    unnamed x12, local copies, waits for them, and re-layouts  3.78 us
    ppermute x2, starting transfers between devices, body(): near.append(lax.ppermute(far[pieces - 1], 'tok', to_even))  2.58 us
    ppermute x4, waiting for transfers between devices, body(): lax.ppermute(own, 'tok', [(i, i + 2 * p) for i in range(shards - 2 * p)])  1.72 us
  transfers between devices with their start and end apart: 16, of which 1 were waited for; matrix products, arithmetic and copies ran while one was open for 5% of the time, Pallas kernels for 16%

profile of v1, /device:TPU:0, one launch (start us, length us, event | category | flops | bytes accessed | tf_op | source)
XLA Modules:
  0.0 78.3 jit_solution(11553110012734383200)
XLA Ops:
  0.6 0.0 copy-start.3
  0.6 0.0 copy-start.4
  0.7 0.1 pad_add_fusion.where_ref
  0.7 0.6 copy-done.3
  1.3 0.0 copy-done.4
  1.3 0.0 copy-start.1
  1.3 0.9 %copy-done.1 = bf16[256,256]{1,0:T(8,128)(2,1)S(1)} copy-done((bf16[256,256]{1,0:T(8,128)(2,1)S(1)}, bf16[256,256]{1,0:T(8,128)(2,1)}, u32[]{:S(2)}) %copy-start.1) | copy-done | bytes 131096
  2.2 0.0 copy-start.2
  2.2 0.9 %copy-done.2 = bf16[256,256]{1,0:T(8,128)(2,1)S(1)} copy-done((bf16[256,256]{1,0:T(8,128)(2,1)S(1)}, bf16[256,256]{1,0:T(8,128)(2,1)}, u32[]{:S(2)}) %copy-start.2) | copy-done | bytes 131096
  3.1 1.3 %rotate_keys.1 = (bf16[256,256]{1,0:T(8,128)(2,1)S(1)}, bf16[256,256]{1,0:T(8,128)(2,1)S(1)}) custom-call(s32[2]{0:T(128)S(1)} %pad_add_fusion.where_ref, s32[16]{0:T(128)S(1)} %copy-done.3, f32[1,128]{1,0:T(1,128)S(1)} %copy-done.4, bf16[256,256]{1,0:T(8,128)(2,1)S(1)} %copy-done.1, bf16[256,256]{1,0:T(8,128)(2,1)S(1)} %copy-done.2), custom_call_target="tpu_custom_call" | custom-call | tf_op jit(solution)/shard_map/rotate_keys/pallas_call | solution.py:231
  4.4 4.8 %collective-permute-start = (bf16[256,256]{1,0:T(8,128)(2,1)S(1)}, bf16[256,256]{1,0:T(8,128)(2,1)S(1)}, u32[]{:S(2)}, u32[]{:S(2)}) collective-permute-start(bf16[256,256]{1,0:T(8,128)(2,1)S(1)} %get-tuple-element.18.refs_0_), channel_id=1, source_target_pairs={{0,8},{4,12},{8,16},{12,20},{16,24},{20,28},{1,9},{5,13},{9,17},{1... | collective-permute-start | bytes 393224 | tf_op jit(solution)/shard_map/ppermute | solution.py:260
  9.3 3.4 %collective-permute-start.1 = (bf16[256,256]{1,0:T(8,128)(2,1)S(1)}, bf16[256,256]{1,0:T(8,128)(2,1)S(1)}, u32[]{:S(2)}, u32[]{:S(2)}) collective-permute-start(bf16[256,256]{1,0:T(8,128)(2,1)S(1)} %get-tuple-element.18.refs_0_), channel_id=1, source_target_pairs={{0,16},{4,20},{8,24},{12,28},{1,17},{5,21},{9,25},{13,29},{2,18},{... | collective-permute-start | bytes 393224 | tf_op jit(solution)/shard_map/ppermute | solution.py:260
  12.7 1.3 %collective-permute-start.2 = (bf16[256,256]{1,0:T(8,128)(2,1)S(1)}, bf16[256,256]{1,0:T(8,128)(2,1)S(1)}, u32[]{:S(2)}, u32[]{:S(2)}) collective-permute-start(bf16[256,256]{1,0:T(8,128)(2,1)S(1)} %get-tuple-element.18.refs_0_), channel_id=1, source_target_pairs={{0,4},{8,12},{16,20},{24,28},{1,5},{9,13},{17,21},{25,29},{2,6},{1... | collective-permute-start | bytes 393224 | tf_op jit(solution)/shard_map/ppermute | solution.py:264
  14.0 0.0 collective-permute-done.refs_1_
  14.0 1.7 %collective-permute-done.1.refs_2_ = bf16[256,256]{1,0:T(8,128)(2,1)S(1)} collective-permute-done((bf16[256,256]{1,0:T(8,128)(2,1)S(1)}, bf16[256,256]{1,0:T(8,128)(2,1)S(1)}, u32[]{:S(2)}, u32[]{:S(2)}) %collective-permute-start.1) | collective-permute-done | bytes 131104 | tf_op jit(solution)/shard_map/ppermute | solution.py:260
  15.7 1.3 %collective-permute-start.5 = (bf16[256,256]{1,0:T(8,128)(2,1)S(1)}, bf16[256,256]{1,0:T(8,128)(2,1)S(1)}, u32[]{:S(2)}, u32[]{:S(2)}) collective-permute-start(bf16[256,256]{1,0:T(8,128)(2,1)S(1)} %get-tuple-element.22.refs_0_), channel_id=1, source_target_pairs={{0,8},{4,12},{8,16},{12,20},{16,24},{20,28},{1,9},{5,13},{9,17},{1... | collective-permute-start | bytes 393224 | tf_op jit(solution)/shard_map/ppermute | solution.py:260
  17.0 5.0 %collective-permute-start.6 = (bf16[256,256]{1,0:T(8,128)(2,1)S(1)}, bf16[256,256]{1,0:T(8,128)(2,1)S(1)}, u32[]{:S(2)}, u32[]{:S(2)}) collective-permute-start(bf16[256,256]{1,0:T(8,128)(2,1)S(1)} %get-tuple-element.22.refs_0_), channel_id=1, source_target_pairs={{0,16},{4,20},{8,24},{12,28},{1,17},{5,21},{9,25},{13,29},{2,18},{... | collective-permute-start | bytes 393224 | tf_op jit(solution)/shard_map/ppermute | solution.py:260
  22.1 0.1 collective-permute-start.3
  22.1 1.3 %collective-permute-start.4 = (bf16[256,256]{1,0:T(8,128)(2,1)S(1)}, bf16[256,256]{1,0:T(8,128)(2,1)S(1)}, u32[]{:S(2)}, u32[]{:S(2)}) collective-permute-start(bf16[256,256]{1,0:T(8,128)(2,1)S(1)} %collective-permute-done.1.refs_2_), channel_id=1, source_target_pairs={{4,0},{12,8},{20,16},{28,24},{5,1},{13,9},{21,17},{29,25},{6,2},{1... | collective-permute-start | bytes 393224 | tf_op jit(solution)/shard_map/ppermute | solution.py:267
  23.4 0.7 fusion
  24.1 0.0 collective-permute-done.2.refs_3_
  24.1 3.0 %collective-permute-start.7 = (bf16[256,256]{1,0:T(8,128)(2,1)S(1)}, bf16[256,256]{1,0:T(8,128)(2,1)S(1)}, u32[]{:S(2)}, u32[]{:S(2)}) collective-permute-start(bf16[256,256]{1,0:T(8,128)(2,1)S(1)} %get-tuple-element.22.refs_0_), channel_id=1, source_target_pairs={{0,4},{8,12},{16,20},{24,28},{1,5},{9,13},{17,21},{25,29},{2,6},{1... | collective-permute-start | bytes 393224 | tf_op jit(solution)/shard_map/ppermute | solution.py:264
  27.2 0.0 collective-permute-done.5.refs_1_
  27.2 0.1 collective-permute-start.8
  27.3 0.0 collective-permute-done.6.refs_2_
  27.3 1.3 %collective-permute-start.9 = (bf16[256,256]{1,0:T(8,128)(2,1)S(1)}, bf16[256,256]{1,0:T(8,128)(2,1)S(1)}, u32[]{:S(2)}, u32[]{:S(2)}) collective-permute-start(bf16[256,256]{1,0:T(8,128)(2,1)S(1)} %collective-permute-done.6.refs_2_), channel_id=1, source_target_pairs={{4,0},{12,8},{20,16},{28,24},{5,1},{13,9},{21,17},{29,25},{6,2},{1... | collective-permute-start | bytes 393224 | tf_op jit(solution)/shard_map/ppermute | solution.py:267
  28.6 0.0 copy-start
  28.6 1.2 %copy-done = bf16[256,2048]{1,0:T(8,128)(2,1)S(1)} copy-done((bf16[256,2048]{1,0:T(8,128)(2,1)S(1)}, bf16[256,2048]{1,0:T(8,128)(2,1)}, u32[]{:S(2)}) %copy-start) | copy-done | bytes 1048600
  29.8 1.7 %rotate_queries.1 = (bf16[4,512,128]{2,1,0:T(8,128)(2,1)S(1)}, bf16[4,512,128]{2,1,0:T(8,128)(2,1)S(1)}) custom-call(s32[2]{0:T(128)S(1)} %pad_add_fusion.where_ref, s32[16]{0:T(128)S(1)} %copy-done.3, f32[1,128]{1,0:T(1,128)S(1)} %copy-done.4, bf16[256,2048]{1,0:T(8,128)(2,1)S(1)} %copy-done), custom_call_target="tpu_custom_call" | custom-call | tf_op jit(solution)/shard_map/rotate_queries/pallas_call | solution.py:239
  31.5 0.0 collective-permute-done.3.refs_4_
  31.5 0.0 collective-permute-done.4.refs_5_
  31.5 5.5 %attend.2 = (bf16[64,1024]{1,0:T(8,128)(2,1)S(1)}, bf16[64,1024]{1,0:T(8,128)(2,1)S(1)}, bf16[64,1024]{1,0:T(8,128)(2,1)S(1)}, bf16[64,1024]{1,0:T(8,128)(2,1)S(1)}, f32[4,64,8]{2,1,0:T(8,128)S(1)}) custom-call(s32[2]{0:T(128)S(1)} %pad_add_fusion.where_ref, s32[16]{0:T(128)S(1)} %copy-done.3, bf16[4,512,128]{2,1,0:T(8,128)(2,1)S(1)} %get-tuple-element.17.query_ref, ...), custom_call_target="tpu_custom_call" | custom-call | tf_op jit(solution)/shard_map/attend/pallas_call | solution.py:269
  37.0 1.6 %collective-permute-start.10 = (bf16[64,1024]{1,0:T(8,128)(2,1)S(1)}, bf16[64,1024]{1,0:T(8,128)(2,1)S(1)}, u32[]{:S(2)}, u32[]{:S(2)}) collective-permute-start(bf16[64,1024]{1,0:T(8,128)(2,1)S(1)} %get-tuple-element.24), channel_id=1, source_target_pairs={{0,1},{1,2},{2,3},{3,0},{4,5},{5,6},{6,7},{7,4},{8,9},{9,10},{10,1... | collective-permute-start | bytes 393224 | tf_op jit(solution)/shard_map/ppermute | solution.py:291
  38.6 0.7 compare_and_fusion
  39.3 2.6 %collective-permute-start.12 = (bf16[64,1024]{1,0:T(8,128)(2,1)S(1)}, bf16[64,1024]{1,0:T(8,128)(2,1)S(1)}, u32[]{:S(2)}, u32[]{:S(2)}) collective-permute-start(bf16[64,1024]{1,0:T(8,128)(2,1)S(1)} %get-tuple-element.26), channel_id=1, source_target_pairs={{0,2},{1,3},{2,0},{3,1},{4,6},{5,7},{6,4},{7,5},{8,10},{9,11},{10,... | collective-permute-start | bytes 393224 | tf_op jit(solution)/shard_map/ppermute | solution.py:291
  41.9 0.1 copy.9
  42.0 0.0 collective-permute-done.7.refs_3_
  42.0 1.4 %collective-permute-start.14 = (bf16[64,1024]{1,0:T(8,128)(2,1)S(1)}, bf16[64,1024]{1,0:T(8,128)(2,1)S(1)}, u32[]{:S(2)}, u32[]{:S(2)}) collective-permute-start(bf16[64,1024]{1,0:T(8,128)(2,1)S(1)} %get-tuple-element.28), channel_id=1, source_target_pairs={{0,3},{1,0},{2,1},{3,2},{4,7},{5,4},{6,5},{7,6},{8,11},{9,8},{10,9... | collective-permute-start | bytes 393224 | tf_op jit(solution)/shard_map/ppermute | solution.py:291
  43.4 0.0 collective-permute-done.8.refs_4_
  43.4 0.0 collective-permute-done.9.refs_5_
  43.4 5.5 %attend.3 = (bf16[64,1024]{1,0:T(8,128)(2,1)S(1)}, bf16[64,1024]{1,0:T(8,128)(2,1)S(1)}, bf16[64,1024]{1,0:T(8,128)(2,1)S(1)}, bf16[64,1024]{1,0:T(8,128)(2,1)S(1)}, f32[4,64,8]{2,1,0:T(8,128)S(1)}) custom-call(s32[2]{0:T(128)S(1)} %pad_add_fusion.where_ref, s32[16]{0:T(128)S(1)} %copy-done.3, bf16[4,512,128]{2,1,0:T(8,128)(2,1)S(1)} %get-tuple-element.20.query_ref, ...), custom_call_target="tpu_custom_call" | custom-call | tf_op jit(solution)/shard_map/attend/pallas_call | solution.py:269
  48.9 0.7 collective-permute-start.11
  49.6 0.4 collective-permute-start.13
  49.9 0.1 copy.10
  50.0 0.6 gather_fusion
  50.6 0.0 collective-permute-done.10.refs_2_
  50.6 2.9 %collective-permute-start.15 = (bf16[64,1024]{1,0:T(8,128)(2,1)S(1)}, bf16[64,1024]{1,0:T(8,128)(2,1)S(1)}, u32[]{:S(2)}, u32[]{:S(2)}) collective-permute-start(bf16[64,1024]{1,0:T(8,128)(2,1)S(1)} %get-tuple-element.29), channel_id=1, source_target_pairs={{0,3},{1,0},{2,1},{3,2},{4,7},{5,4},{6,5},{7,6},{8,11},{9,8},{10,9... | collective-permute-start | bytes 393224 | tf_op jit(solution)/shard_map/ppermute | solution.py:291
  53.5 0.1 fusion.1
  53.6 0.1 reshape.57
  53.7 21.1 %all_to_all.5 = f32[8,1,512]{2,1,0:T(1,128)S(1)} all-to-all(f32[8,1,512]{2,1,0:T(1,128)S(1)} %reshape.57), channel_id=1, replica_groups=mesh['tok'=8,'kv'=4] {'tok'}, dimensions={0} | all-to-all | bytes 32768 | tf_op jit(solution)/shard_map/all_to_all | solution.py:311
  74.7 0.5 broadcast.36
  75.2 0.7 reduce
  75.9 0.1 reshape.58
  76.0 0.7 reshape.48
  76.7 0.0 collective-permute-done.12.refs_4_
  76.7 0.0 collective-permute-done.14.refs_6_
  76.7 0.0 collective-permute-done.11.refs_3_
  76.7 0.0 collective-permute-done.13.refs_5_
  76.8 0.0 collective-permute-done.15.refs_7_
  76.8 1.6 %assemble.1 = bf16[64,8192]{1,0:T(8,128)(2,1)} custom-call(s32[2]{0:T(128)S(1)} %pad_add_fusion.where_ref, bf16[64,1024]{1,0:T(8,128)(2,1)S(1)} %get-tuple-element.19.refs_0_, bf16[64,1024]{1,0:T(8,128)(2,1)S(1)} %get-tuple-element.23.refs_1_, bf16[64,1024]{1,0:T(8,128)(2,1)S(1)} %collective-permute-done.10.refs_2_, ...), custom_call_target="tpu_custom_call" | custom-call | tf_op jit(solution)/shard_map/assemble/pallas_call | solution.py:298
  (3 shorter events, 0.0 us)
Async XLA Ops:
  0.6 0.7 copy-start.3
  0.6 0.7 copy-start.4
  1.3 0.9 %copy-start.1 = (bf16[256,256]{1,0:T(8,128)(2,1)S(1)}, bf16[256,256]{1,0:T(8,128)(2,1)}, u32[]{:S(2)}) copy-start(bf16[256,256]{1,0:T(8,128)(2,1)} %key_ref.1) | copy-start | bytes 393220
  2.2 0.9 %copy-start.2 = (bf16[256,256]{1,0:T(8,128)(2,1)S(1)}, bf16[256,256]{1,0:T(8,128)(2,1)}, u32[]{:S(2)}) copy-start(bf16[256,256]{1,0:T(8,128)(2,1)} %value_ref.1) | copy-start | bytes 393220
  4.4 9.6 %collective-permute-start = (bf16[256,256]{1,0:T(8,128)(2,1)S(1)}, bf16[256,256]{1,0:T(8,128)(2,1)S(1)}, u32[]{:S(2)}, u32[]{:S(2)}) collective-permute-start(bf16[256,256]{1,0:T(8,128)(2,1)S(1)} %get-tuple-element.18.refs_0_), channel_id=1, source_target_pairs={{0,8},{4,12},{8,16},{12,20},{16,24},{20,28},{1,9},{5,13},{9,17},{1... | collective-permute-start | bytes 393224 | tf_op jit(solution)/shard_map/ppermute | solution.py:260
  9.3 6.5 %collective-permute-start.1 = (bf16[256,256]{1,0:T(8,128)(2,1)S(1)}, bf16[256,256]{1,0:T(8,128)(2,1)S(1)}, u32[]{:S(2)}, u32[]{:S(2)}) collective-permute-start(bf16[256,256]{1,0:T(8,128)(2,1)S(1)} %get-tuple-element.18.refs_0_), channel_id=1, source_target_pairs={{0,16},{4,20},{8,24},{12,28},{1,17},{5,21},{9,25},{13,29},{2,18},{... | collective-permute-start | bytes 393224 | tf_op jit(solution)/shard_map/ppermute | solution.py:260
  12.7 11.4 %collective-permute-start.2 = (bf16[256,256]{1,0:T(8,128)(2,1)S(1)}, bf16[256,256]{1,0:T(8,128)(2,1)S(1)}, u32[]{:S(2)}, u32[]{:S(2)}) collective-permute-start(bf16[256,256]{1,0:T(8,128)(2,1)S(1)} %get-tuple-element.18.refs_0_), channel_id=1, source_target_pairs={{0,4},{8,12},{16,20},{24,28},{1,5},{9,13},{17,21},{25,29},{2,6},{1... | collective-permute-start | bytes 393224 | tf_op jit(solution)/shard_map/ppermute | solution.py:264
  15.7 11.4 %collective-permute-start.5 = (bf16[256,256]{1,0:T(8,128)(2,1)S(1)}, bf16[256,256]{1,0:T(8,128)(2,1)S(1)}, u32[]{:S(2)}, u32[]{:S(2)}) collective-permute-start(bf16[256,256]{1,0:T(8,128)(2,1)S(1)} %get-tuple-element.22.refs_0_), channel_id=1, source_target_pairs={{0,8},{4,12},{8,16},{12,20},{16,24},{20,28},{1,9},{5,13},{9,17},{1... | collective-permute-start | bytes 393224 | tf_op jit(solution)/shard_map/ppermute | solution.py:260
  17.0 10.2 %collective-permute-start.6 = (bf16[256,256]{1,0:T(8,128)(2,1)S(1)}, bf16[256,256]{1,0:T(8,128)(2,1)S(1)}, u32[]{:S(2)}, u32[]{:S(2)}) collective-permute-start(bf16[256,256]{1,0:T(8,128)(2,1)S(1)} %get-tuple-element.22.refs_0_), channel_id=1, source_target_pairs={{0,16},{4,20},{8,24},{12,28},{1,17},{5,21},{9,25},{13,29},{2,18},{... | collective-permute-start | bytes 393224 | tf_op jit(solution)/shard_map/ppermute | solution.py:260
  22.1 9.5 %collective-permute-start.3 = (bf16[256,256]{1,0:T(8,128)(2,1)S(1)}, bf16[256,256]{1,0:T(8,128)(2,1)S(1)}, u32[]{:S(2)}, u32[]{:S(2)}) collective-permute-start(bf16[256,256]{1,0:T(8,128)(2,1)S(1)} %collective-permute-done.refs_1_), channel_id=1, source_target_pairs={{0,4},{4,0},{8,12},{12,8},{16,20},{20,16},{24,28},{28,24},{1,5},{5... | collective-permute-start | bytes 393224 | tf_op jit(solution)/shard_map/ppermute | solution.py:266
  22.1 9.4 %collective-permute-start.4 = (bf16[256,256]{1,0:T(8,128)(2,1)S(1)}, bf16[256,256]{1,0:T(8,128)(2,1)S(1)}, u32[]{:S(2)}, u32[]{:S(2)}) collective-permute-start(bf16[256,256]{1,0:T(8,128)(2,1)S(1)} %collective-permute-done.1.refs_2_), channel_id=1, source_target_pairs={{4,0},{12,8},{20,16},{28,24},{5,1},{13,9},{21,17},{29,25},{6,2},{1... | collective-permute-start | bytes 393224 | tf_op jit(solution)/shard_map/ppermute | solution.py:267
  24.1 17.9 %collective-permute-start.7 = (bf16[256,256]{1,0:T(8,128)(2,1)S(1)}, bf16[256,256]{1,0:T(8,128)(2,1)S(1)}, u32[]{:S(2)}, u32[]{:S(2)}) collective-permute-start(bf16[256,256]{1,0:T(8,128)(2,1)S(1)} %get-tuple-element.22.refs_0_), channel_id=1, source_target_pairs={{0,4},{8,12},{16,20},{24,28},{1,5},{9,13},{17,21},{25,29},{2,6},{1... | collective-permute-start | bytes 393224 | tf_op jit(solution)/shard_map/ppermute | solution.py:264
  27.2 16.2 %collective-permute-start.8 = (bf16[256,256]{1,0:T(8,128)(2,1)S(1)}, bf16[256,256]{1,0:T(8,128)(2,1)S(1)}, u32[]{:S(2)}, u32[]{:S(2)}) collective-permute-start(bf16[256,256]{1,0:T(8,128)(2,1)S(1)} %collective-permute-done.5.refs_1_), channel_id=1, source_target_pairs={{0,4},{4,0},{8,12},{12,8},{16,20},{20,16},{24,28},{28,24},{1,5},{5... | collective-permute-start | bytes 393224 | tf_op jit(solution)/shard_map/ppermute | solution.py:266
  27.3 16.1 %collective-permute-start.9 = (bf16[256,256]{1,0:T(8,128)(2,1)S(1)}, bf16[256,256]{1,0:T(8,128)(2,1)S(1)}, u32[]{:S(2)}, u32[]{:S(2)}) collective-permute-start(bf16[256,256]{1,0:T(8,128)(2,1)S(1)} %collective-permute-done.6.refs_2_), channel_id=1, source_target_pairs={{4,0},{12,8},{20,16},{28,24},{5,1},{13,9},{21,17},{29,25},{6,2},{1... | collective-permute-start | bytes 393224 | tf_op jit(solution)/shard_map/ppermute | solution.py:267
  28.6 1.2 %copy-start = (bf16[256,2048]{1,0:T(8,128)(2,1)S(1)}, bf16[256,2048]{1,0:T(8,128)(2,1)}, u32[]{:S(2)}) copy-start(bf16[256,2048]{1,0:T(8,128)(2,1)} %query_ref.1) | copy-start | bytes 3145732
  37.0 13.6 %collective-permute-start.10 = (bf16[64,1024]{1,0:T(8,128)(2,1)S(1)}, bf16[64,1024]{1,0:T(8,128)(2,1)S(1)}, u32[]{:S(2)}, u32[]{:S(2)}) collective-permute-start(bf16[64,1024]{1,0:T(8,128)(2,1)S(1)} %get-tuple-element.24), channel_id=1, source_target_pairs={{0,1},{1,2},{2,3},{3,0},{4,5},{5,6},{6,7},{7,4},{8,9},{9,10},{10,1... | collective-permute-start | bytes 393224 | tf_op jit(solution)/shard_map/ppermute | solution.py:291
  39.3 37.4 %collective-permute-start.12 = (bf16[64,1024]{1,0:T(8,128)(2,1)S(1)}, bf16[64,1024]{1,0:T(8,128)(2,1)S(1)}, u32[]{:S(2)}, u32[]{:S(2)}) collective-permute-start(bf16[64,1024]{1,0:T(8,128)(2,1)S(1)} %get-tuple-element.26), channel_id=1, source_target_pairs={{0,2},{1,3},{2,0},{3,1},{4,6},{5,7},{6,4},{7,5},{8,10},{9,11},{10,... | collective-permute-start | bytes 393224 | tf_op jit(solution)/shard_map/ppermute | solution.py:291
  42.0 34.7 %collective-permute-start.14 = (bf16[64,1024]{1,0:T(8,128)(2,1)S(1)}, bf16[64,1024]{1,0:T(8,128)(2,1)S(1)}, u32[]{:S(2)}, u32[]{:S(2)}) collective-permute-start(bf16[64,1024]{1,0:T(8,128)(2,1)S(1)} %get-tuple-element.28), channel_id=1, source_target_pairs={{0,3},{1,0},{2,1},{3,2},{4,7},{5,4},{6,5},{7,6},{8,11},{9,8},{10,9... | collective-permute-start | bytes 393224 | tf_op jit(solution)/shard_map/ppermute | solution.py:291
  48.9 27.9 %collective-permute-start.11 = (bf16[64,1024]{1,0:T(8,128)(2,1)S(1)}, bf16[64,1024]{1,0:T(8,128)(2,1)S(1)}, u32[]{:S(2)}, u32[]{:S(2)}) collective-permute-start(bf16[64,1024]{1,0:T(8,128)(2,1)S(1)} %get-tuple-element.25), channel_id=1, source_target_pairs={{0,1},{1,2},{2,3},{3,0},{4,5},{5,6},{6,7},{7,4},{8,9},{9,10},{10,1... | collective-permute-start | bytes 393224 | tf_op jit(solution)/shard_map/ppermute | solution.py:291
  49.6 27.2 %collective-permute-start.13 = (bf16[64,1024]{1,0:T(8,128)(2,1)S(1)}, bf16[64,1024]{1,0:T(8,128)(2,1)S(1)}, u32[]{:S(2)}, u32[]{:S(2)}) collective-permute-start(bf16[64,1024]{1,0:T(8,128)(2,1)S(1)} %get-tuple-element.27), channel_id=1, source_target_pairs={{0,2},{1,3},{2,0},{3,1},{4,6},{5,7},{6,4},{7,5},{8,10},{9,11},{10,... | collective-permute-start | bytes 393224 | tf_op jit(solution)/shard_map/ppermute | solution.py:291
  50.6 26.1 %collective-permute-start.15 = (bf16[64,1024]{1,0:T(8,128)(2,1)S(1)}, bf16[64,1024]{1,0:T(8,128)(2,1)S(1)}, u32[]{:S(2)}, u32[]{:S(2)}) collective-permute-start(bf16[64,1024]{1,0:T(8,128)(2,1)S(1)} %get-tuple-element.29), channel_id=1, source_target_pairs={{0,3},{1,0},{2,1},{3,2},{4,7},{5,4},{6,5},{7,6},{8,11},{9,8},{10,9... | collective-permute-start | bytes 393224 | tf_op jit(solution)/shard_map/ppermute | solution.py:291
